TPU v7x, 512 devices: a whole 4x8x8 slice. The times are simulated.
512 devices in a mesh: lon: 32 (over x, z_hi, core), lat: 16 (over y, z_lo).
Axes of the slice: x: 4, y: 8, z: 8 (z_hi: 4, z_lo: 2; z = z_hi * 2 + z_lo), core: 2. Of those that a mesh axis runs over, the one named last changes fastest.
Arguments:
- fields: bfloat16 [1, 64, 256, 4096], P(None, None, 'lat', 'lon'), may hold values from -6 to 6
- cotangent: bfloat16 [1, 64, 256, 4096], P(None, None, 'lat', 'lon'), may hold values from -6 to 6
- ocean_mask: int32 [256, 4096], P('lat', 'lon'), may hold values 0 or 1
- seam_partner: int32 [4096], replicated, may hold values from 0 to 4095, as said below
- depth_weight: bfloat16 [64, 7, 7], replicated, may hold values from -0.875 to 0.875
- norm_gain: bfloat16 [64], replicated, may hold values from 0.5 to 1.5
- layer_norm_bias: bfloat16 [64], replicated, may hold values from -3 to 3
- up_weight: bfloat16 [256, 64], replicated, may hold values from -0.75 to 0.75
- up_bias: bfloat16 [256], replicated, may hold values from -3 to 3
- down_weight: bfloat16 [64, 256], replicated, may hold values from -0.375 to 0.375
- layer_scale: bfloat16 [64], replicated, may hold values from 0.5 to 1.5
Outputs:
- output: bfloat16 [1, 64, 256, 4096], P(None, None, 'lat', 'lon')
- grad_fields: bfloat16 [1, 64, 256, 4096], P(None, None, 'lat', 'lon')
- grad_depth: float32 [64, 7, 7], replicated
- grad_gain: float32 [64], replicated
- grad_bias: float32 [64], replicated
- grad_up_weight: float32 [256, 64], replicated
- grad_up_bias: float32 [256], replicated
- grad_down_weight: float32 [64, 256], replicated
- grad_scale: float32 [64], replicated
Inputs may be any that keep to these rules, and one draw needn't show every extreme that they name: seam_partner[i] = (s - i) mod 4096 for one whole number s, so it is its own inverse.
All inputs are finite; a program needn't handle non-finite values. No bound on the sum of `ocean_mask` on one device may be relied on, other than what follows from the above.
Results may differ from a plain program's by a relative error of at most 0.0068.
Values may be sent and summed in bfloat16 or wider, within the bound.
A program may use at most 64 MiB of HBM per device.

v0:
```python
import math
import jax
import jax.numpy as jnp
from jax import lax
from jax.sharding import PartitionSpec as P


def extended_2(cells, sides, width, closed):
    for axis, dim in sides:
        count = lax.axis_size(axis)
        ends = count if closed else count - 1
        head = lax.slice_in_dim(cells, 0, width, axis=dim)
        tail = lax.slice_in_dim(cells, cells.shape[dim] - width, cells.shape[dim], axis=dim)
        cells = jnp.concatenate(
            [
                lax.ppermute(tail, axis, [(i, (i + 1) % count) for i in range(ends)]),
                cells,
                lax.ppermute(head, axis, [((i + 1) % count, i) for i in range(ends)]),
            ],
            axis=dim,
        )
    return cells


def gelu_slope(pre):
    cdf = 0.5 * (1.0 + lax.erf(pre / math.sqrt(2.0)))
    return cdf + pre * jnp.exp(-0.5 * pre * pre) / math.sqrt(2.0 * math.pi)


def cell_terms(
    conv, field, cot, mask, norm_gain, layer_norm_bias, up_weight, up_bias, down_weight, layer_scale
):
    mean_c = jnp.mean(conv, axis=0, keepdims=True)
    centered_input = conv - mean_c
    var_c = jnp.mean(centered_input * centered_input, axis=0, keepdims=True)
    reciprocal_deviation = lax.rsqrt(var_c + 1e-06)
    standardized_input = centered_input * reciprocal_deviation
    layer_norm_gain = norm_gain.astype(jnp.float32)[:, None]
    normalized_output = (
        standardized_input * layer_norm_gain + layer_norm_bias.astype(jnp.float32)[:, None]
    ).astype(jnp.bfloat16)
    pre = (
        jnp.dot(up_weight, normalized_output, preferred_element_type=jnp.float32)
        + up_bias.astype(jnp.float32)[:, None]
    )
    hidden = jax.nn.gelu(pre, approximate=False).astype(jnp.bfloat16)
    branch = jnp.dot(down_weight, hidden, preferred_element_type=jnp.float32)
    scale = layer_scale.astype(jnp.float32)[:, None]
    out = (mask * (field.astype(jnp.float32) + scale * branch)).astype(jnp.bfloat16)
    grad_in = mask * cot.astype(jnp.float32)
    d_branch = (grad_in * scale).astype(jnp.bfloat16)
    g_scale = jnp.sum(grad_in * branch, axis=1)
    contract_cells = (((1,), (1,)), ((), ()))
    contract_first = (((0,), (0,)), ((), ()))
    g_down = lax.dot_general(d_branch, hidden, contract_cells, preferred_element_type=jnp.float32)
    d_hidden = lax.dot_general(
        down_weight, d_branch, contract_first, preferred_element_type=jnp.float32
    )
    d_pre = (d_hidden * gelu_slope(pre)).astype(jnp.bfloat16)
    g_up_b = jnp.sum(d_pre.astype(jnp.float32), axis=1)
    g_up_w = lax.dot_general(
        d_pre, normalized_output, contract_cells, preferred_element_type=jnp.float32
    )
    normalized_gradient = lax.dot_general(
        up_weight, d_pre, contract_first, preferred_element_type=jnp.float32
    )
    gain_gradient = jnp.sum(normalized_gradient * standardized_input, axis=1)
    g_bias = jnp.sum(normalized_gradient, axis=1)
    gradient_through_norm = normalized_gradient * layer_norm_gain
    convolution_gradient = reciprocal_deviation * (
        gradient_through_norm
        - jnp.mean(gradient_through_norm, axis=0, keepdims=True)
        - standardized_input
        * jnp.mean(gradient_through_norm * standardized_input, axis=0, keepdims=True)
    )
    return (
        out,
        convolution_gradient.astype(jnp.bfloat16),
        (gain_gradient, g_bias, g_up_w, g_up_b, g_down, g_scale),
    )


def make_picker(wanted, carry, piece):
    width = piece.shape[3]
    inside = (wanted >= 0) & (wanted < width)
    picked = jnp.take(piece, jnp.clip(wanted, 0, width - 1), axis=3)
    return jnp.where(inside[None, None, None, :], picked, carry)


def shards(
    fields,
    cotangent,
    ocean_mask,
    seam_partner,
    depth_weight,
    norm_gain,
    layer_norm_bias,
    up_weight,
    up_bias,
    down_weight,
    layer_scale,
):
    samples, chans, rows, cols = fields.shape
    total_lon = seam_partner.shape[0]
    lon_start = lax.axis_index("lon") * cols
    positions = (lon_start + jnp.arange(-3, cols + 3, dtype=jnp.int32)) % total_lon
    partner_cols = jnp.take(seam_partner, positions)
    own_partner = partner_cols[3 : cols + 3]
    is_top = lax.axis_index("lat") == lax.axis_size("lat") - 1
    weight_f = depth_weight.astype(jnp.float32)
    mask_f = ocean_mask.astype(jnp.float32)
    lon_padded = extended_2(fields, (("lon", 3),), 3, True)
    banded = extended_2(lon_padded, (("lat", 2),), 3, False)
    upper = fields[:, :, rows - 3 :, :][:, :, ::-1, :]
    fold_init = jnp.zeros((samples, chans, 3, cols + 6), jnp.bfloat16)
    folded = make_picker(partner_cols, fold_init, lax.all_gather(upper, "lon", axis=3, tiled=True))
    top_rows = jnp.where(is_top, folded, banded[:, :, rows + 3 :, :])
    extended = jnp.concatenate([banded[:, :, : rows + 3, :], top_rows], axis=2)
    conv = jnp.zeros((samples, chans, rows, cols), jnp.float32)
    for row_tap in range(7):
        for col_tap in range(7):
            conv = conv + weight_f[:, row_tap, col_tap][None, :, None, None] * extended[
                :, :, row_tap : row_tap + rows, col_tap : col_tap + cols
            ].astype(jnp.float32)
    mask_flat = mask_f.reshape(1, rows * cols)
    out_s, dconv_s, parts = cell_terms(
        conv[0].reshape(chans, rows * cols),
        fields[0].reshape(chans, rows * cols),
        cotangent[0].reshape(chans, rows * cols),
        mask_flat,
        norm_gain,
        layer_norm_bias,
        up_weight,
        up_bias,
        down_weight,
        layer_scale,
    )
    outputs = [out_s.reshape(chans, rows, cols)]
    dconv_list = [dconv_s.reshape(chans, rows, cols)]
    output = jnp.stack(outputs)
    convolution_gradient = jnp.stack(dconv_list)
    d_conv_f = convolution_gradient.astype(jnp.float32)
    taps = []
    for row_tap in range(7):
        line = []
        for col_tap in range(7):
            line.append(
                jnp.sum(
                    d_conv_f
                    * extended[:, :, row_tap : row_tap + rows, col_tap : col_tap + cols].astype(
                        jnp.float32
                    ),
                    axis=(0, 2, 3),
                )
            )
        taps.append(jnp.stack(line, axis=1))
    g_depth = jnp.stack(taps, axis=1)
    lon_back = extended_2(convolution_gradient, (("lon", 3),), 3, True)
    band_back = extended_2(lon_back, (("lat", 2),), 3, False)
    deeper = jnp.pad(band_back, ((0, 0), (0, 0), (0, 3), (0, 0)))
    spread = jnp.zeros((samples, chans, rows + 3, cols), jnp.float32)
    for row_tap in range(7):
        for col_tap in range(7):
            spread = spread + weight_f[:, row_tap, col_tap][None, :, None, None] * deeper[
                :, :, 6 - row_tap : 9 - row_tap + rows, 6 - col_tap : 6 - col_tap + cols
            ].astype(jnp.float32)
    own = spread[:, :, :rows, :]
    margin = spread[:, :, rows:, :]
    back_init = jnp.zeros((samples, chans, 3, cols), jnp.float32)
    back = make_picker(
        own_partner,
        back_init,
        lax.all_gather(margin.astype(jnp.bfloat16), "lon", axis=3, tiled=True).astype(jnp.float32),
    )
    extra = back[:, :, ::-1, :]
    own = own.at[:, :, rows - 3 :, :].add(jnp.where(is_top, extra, 0.0))
    grad_fields = (mask_f[None, None] * cotangent.astype(jnp.float32) + own).astype(jnp.bfloat16)
    gain_gradient, g_bias, g_up_w, g_up_b, g_down, g_scale = parts
    summed = lax.psum(
        (g_depth, gain_gradient, g_bias, g_up_w, g_up_b, g_down, g_scale), ("lon", "lat")
    )
    return (
        output,
        grad_fields,
        summed[0],
        summed[1],
        summed[2],
        summed[3],
        summed[4],
        summed[5],
        summed[6],
    )


def solution(mesh):
    placed = (
        P(None, None, "lat", "lon"),
        P(None, None, "lat", "lon"),
        P("lat", "lon"),
        P(),
        P(),
        P(),
        P(),
        P(),
        P(),
        P(),
        P(),
    )
    return jax.shard_map(
        shards,
        mesh=mesh,
        in_specs=placed,
        out_specs=(
            P(None, None, "lat", "lon"),
            P(None, None, "lat", "lon"),
            P(),
            P(),
            P(),
            P(),
            P(),
            P(),
            P(),
        ),
        check_vma=False,
    )
```

profile of v0, /device:TPU:1, one launch (start us, length us, event | category | flops | bytes accessed | tf_op | source)
XLA Modules:
  0.0 497.8 jit_solution(14033838073368291433)
XLA Ops:
  7.3 1.0 slice.730
  8.3 0.6 rev.6
  9.0 1.5 copy.94
  10.5 7.2 %collective-permute-start = (bf16[1,64,16,3]{1,2,3,0:T(8,128)(2,1)S(1)}, bf16[1,64,16,3]{1,2,3,0:T(8,128)(2,1)S(1)}, u32[]{:S(2)}, u32[]{:S(2)}) collective-permute-start(bf16[1,64,16,3]{1,2,3,0:T(8,128)(2,1)S(1)} %get-tuple-element.147), channel_id=1, source_target_pairs={{0,16},{16,32},{32,48},{48,64},{64,80},{80,96},{96,112},{112,128},... | collective-permute-start | bytes 18440 | tf_op jit(solution)/shard_map/ppermute | solution.py:16
  17.7 3.5 collective-permute-start.1
  21.3 0.7 convert_element_type.421
  22.0 2.0 gather_fusion
  24.0 0.7 compare_and_fusion
  24.8 0.6 slice_bitcast_fusion.48
  25.5 0.7 slice_bitcast_fusion.47
  26.2 0.6 fusion.138
  27.0 1.3 collective-permute-start.3
  28.3 0.6 pad_clamp_fusion
  28.9 1.4 copy.95
  30.3 0.5 convert_element_type.471
  31.3 0.6 convert_element_type.474
  31.9 1.1 copy.108
  33.5 4.2 collective-permute-start.2
  37.7 42.1 %all-gather.3.cloned.1.call-done = bf16[1,64,3,4096]{3,1,2,0:T(8,128)(2,1)} async-done(((bf16[1,64,3,128]{3,1,2,0:T(8,128)(2,1)}), bf16[1,64,3,4096]{3,1,2,0:T(8,128)(2,1)}) %all-gather.3.cloned.1.call-update) | async-done | bytes 1572880 | tf_op jit(solution)/shard_map/all_gather | solution.py:116
  79.8 6.4 %copy.102 = bf16[1,64,3,4096]{1,2,3,0:T(4,128)(2,1)} copy(bf16[1,64,3,4096]{3,1,2,0:T(8,128)(2,1)} %all-gather.3.cloned.1.call-done) | data formatting | bytes 3145728 | tf_op jit(solution)/shard_map/all_gather | solution.py:116
  86.2 3.0 gather_fusion.1
  90.4 10.0 %fusion.134 = (f32[16,128]{0,1:T(8,128)S(1)}, f32[1,64,16,128]{1,2,3,0:T(8,128)S(1)}) fusion(bf16[1,64,19,134]{1,2,3,0:T(8,128)(2,1)S(1)} %get-tuple-element.142, f32[64]{0:T(128)S(1)} %get-tuple-element.152, f32[64]{0:T(128)S(1)} %get-tuple-element.153, f32[64]{0:T(128)S(1)} %get-tuple-element.154, f32[64]{0:T(128)S(1)} %get-tuple-element.155, ...), kind=kLoop, calls=%fused_computation.375 | loop fusion | flops 20051968 | bytes 11829504 | tf_op jit(solution)/shard_map/reduce_sum | solution.py:33
  100.4 1.3 copy.103
  101.9 0.7 multiply_reduce_fusion
  102.8 6.9 %fusion.5 = (bf16[256,2048]{0,1:T(8,128)(2,1)}, f32[256,2048]{0,1:T(8,128)S(1)}) fusion(f32[256]{0:T(256)S(1)} %copy-done.99, bf16[256,64]{0,1:T(8,128)(2,1)S(1)} %copy-done, f32[64]{0:T(128)S(1)} %copy-done.94, f32[64]{0:T(128)S(1)} %copy-done.85, f32[2048]{0:T(1024)S(1)} %rsqrt_bitcast_fusion, f32[2048]{0:T(1024)S(1)} %get-tuple-element.202, ...), kind=kOutput, calls=%fused_computation.63 | convolution fusion | flops 102367232 | bytes 3720704 | tf_op jit(solution)/shard_map/dot_general | solution.py:43
  109.7 2.0 convert_reduce_fusion
  111.7 1.1 fusion.121
  113.6 0.7 copy-done.12
  114.3 0.5 copy.114
  114.9 1.0 copy.109
  115.9 4.1 fusion.113
  120.2 3.2 collective-permute-start.4
  123.4 2.1 collective-permute-start.5
  125.5 1.6 fusion.112
  127.1 7.3 %collective-permute-done.5 = bf16[1,64,16,3]{3,1,2,0:T(8,128)(2,1)S(1)} collective-permute-done((bf16[1,64,16,3]{3,1,2,0:T(8,128)(2,1)S(1)}, bf16[1,64,16,3]{3,1,2,0:T(8,128)(2,1)S(1)}, u32[]{:S(2)}, u32[]{:S(2)}) %collective-permute-start.5) | collective-permute-done | bytes 6176 | tf_op jit(solution)/shard_map/ppermute | solution.py:18
  134.4 0.8 pad_maximum_fusion.8
  135.2 1.9 collective-permute-start.6
  137.2 1.3 collective-permute-start.7
  138.5 1.2 multiply_reduce_fusion.1
  139.7 0.7 reduce_sum.567
  140.3 0.7 copy.119
  141.3 1.3 stack.253
  142.6 1.3 stack.244
  143.9 1.3 stack.235
  145.2 1.4 pad_maximum_fusion.1
  146.7 1.8 pad_maximum_fusion.2
  148.7 6.7 %multiply_add_fusion = f32[1,64,19,128]{3,1,2,0:T(8,128)S(1)} fusion(bf16[1,64,19,134]{3,1,2,0:T(8,128)(2,1)S(1)} %get-tuple-element.138, bf16[1,64,22,134]{3,1,2,0:T(8,128)(2,1)S(1)} %pad_maximum_fusion.1, bf16[1,64,19,134]{3,1,2,0:T(8,128)(2,1)S(1)} %get-tuple-element.137, f32[64]{0:T(128)S(1)} %copy-done.53, f32[64]{0:T(128)S(1)} %copy-done.55, ...), kind=kLoop, calls=%fused_computation.239 | loop fusion | flops 22724608 | bytes 10078720 | tf_op jit(solution)/shard_map/add | solution.py:164
  155.4 0.9 copy-done.10
  156.3 0.6 slice.1226
  157.0 1.2 fusion.92
  158.3 3.9 fusion.85
  162.2 0.7 stack.217
  163.0 0.7 stack.208
  163.7 0.7 stack.199
  164.5 1.7 fusion.132
  166.1 2.3 fusion.133
  168.5 107.1 %all-reduce.1 = (f32[64,7,7]{0,2,1:T(8,128)}, f32[64]{0:T(128)}, f32[64]{0:T(128)}, f32[256]{0:T(256)}, f32[64]{0:T(128)}) all-reduce(f32[64,7,7]{0,2,1:T(8,128)S(1)} %constant_dynamic-update-slice_fusion, f32[64]{0:T(128)S(1)} %copy-done.92, f32[64]{0:T(128)S(1)} %copy-done.91, ...), channel_id=1, replica_groups=mesh['lon'=32,'lat'=16] {'lon','lat'}, use_global_device_ids=true, to_apply=%region_53.54 | all-reduce | flops 3584 | bytes 28672 | tf_op jit(solution)/shard_map/psum | solution.py:179
  275.6 6.4 %copy.112 = bf16[1,64,3,4096]{1,2,3,0:T(4,128)(2,1)} copy(bf16[1,64,3,4096]{3,1,2,0:T(8,128)(2,1)} %all-gather.5.cloned.1.call-done) | data formatting | bytes 3145728 | tf_op jit(solution)/shard_map/all_gather | solution.py:173
  282.1 6.3 %bitcast_convert_fusion = f32[64,3,4096]{0,1,2:T(4,128)} fusion(bf16[1,64,3,4096]{1,2,3,0:T(4,128)(2,1)} %copy.112), kind=kLoop, calls=%fused_computation.52 | loop fusion | flops 786432 | bytes 4718592 | tf_op jit(solution)/shard_map/convert_element_type | solution.py:173
  288.3 4.3 gather_fusion.2
  292.9 0.9 copy.115
  293.8 194.5 %all-reduce.5.cloned.1.call-done = (f32[256,64]{0,1:T(8,128)}, f32[64,256]{1,0:T(8,128)}) async-done(((f32[256,64]{0,1:T(8,128)}, f32[64,256]{1,0:T(8,128)}), (f32[256,64]{0,1:T(8,128)}, f32[64,256]{1,0:T(8,128)})) %all-reduce.5.cloned.1.call-update) | async-done | bytes 131088 | tf_op jit(solution)/shard_map/psum | solution.py:179
  488.3 1.5 copy.159
  489.8 1.5 copy.160
  (250 shorter events, 4.2 us)
Async XLA Ops:
  7.2 95.5 %copy-start = (bf16[256,64]{0,1:T(8,128)(2,1)S(1)}, bf16[256,64]{0,1:T(8,128)(2,1)}, u32[]{:S(2)}) copy-start(bf16[256,64]{0,1:T(8,128)(2,1)} %param.20) | copy-start | bytes 98308
  7.2 19.0 %copy-start.27 = (s32[16,128]{1,0:T(8,128)S(1)}, s32[16,128]{1,0:T(8,128)}, u32[]{:S(2)}) copy-start(s32[16,128]{1,0:T(8,128)} %param.15) | copy-start | bytes 24580
  7.2 19.6 %copy-start.16 = (bf16[1,64,16,128]{3,2,1,0:T(8,128)(2,1)S(1)}, bf16[1,64,16,128]{3,2,1,0:T(8,128)(2,1)}, u32[]{:S(2)}) copy-start(bf16[1,64,16,128]{3,2,1,0:T(8,128)(2,1)} %param.14) | copy-start | bytes 786436
  7.2 72.6 %all-gather.3.cloned.1.call-start = ((), (), s32[]{:S(2)}) async-start(), calls=%async_computation | async-start | bytes 1622016 | tf_op jit(solution)/shard_map/all_gather | solution.py:116
  8.9 266.7 %all-gather.5.cloned.1.call-start = ((), (), s32[]{:S(2)}) async-start(), calls=%async_computation.1 | async-start | bytes 1622016 | tf_op jit(solution)/shard_map/all_gather | solution.py:173
  10.5 19.8 %copy-start.95 = (bf16[64]{0:T(256)(128)(2,1)S(1)}, bf16[64]{0:T(256)(128)(2,1)}, u32[]{:S(2)}) copy-start(bf16[64]{0:T(256)(128)(2,1)} %param.18) | copy-start | bytes 388
  10.5 20.3 %copy-start.96 = (bf16[64]{0:T(256)(128)(2,1)S(1)}, bf16[64]{0:T(256)(128)(2,1)}, u32[]{:S(2)}) copy-start(bf16[64]{0:T(256)(128)(2,1)} %param.19) | copy-start | bytes 388
  10.5 20.8 %copy-start.97 = (bf16[256]{0:T(256)(128)(2,1)S(1)}, bf16[256]{0:T(256)(128)(2,1)}, u32[]{:S(2)}) copy-start(bf16[256]{0:T(256)(128)(2,1)} %param.21) | copy-start | bytes 1540
  10.5 16.3 %collective-permute-start = (bf16[1,64,16,3]{1,2,3,0:T(8,128)(2,1)S(1)}, bf16[1,64,16,3]{1,2,3,0:T(8,128)(2,1)S(1)}, u32[]{:S(2)}, u32[]{:S(2)}) collective-permute-start(bf16[1,64,16,3]{1,2,3,0:T(8,128)(2,1)S(1)} %get-tuple-element.147), channel_id=1, source_target_pairs={{0,16},{16,32},{32,48},{48,64},{64,80},{80,96},{96,112},{112,128},... | collective-permute-start | bytes 18440 | tf_op jit(solution)/shard_map/ppermute | solution.py:16
  17.7 9.1 %collective-permute-start.1 = (bf16[1,64,16,3]{1,2,3,0:T(8,128)(2,1)S(1)}, bf16[1,64,16,3]{1,2,3,0:T(8,128)(2,1)S(1)}, u32[]{:S(2)}, u32[]{:S(2)}) collective-permute-start(bf16[1,64,16,3]{1,2,3,0:T(8,128)(2,1)S(1)} %get-tuple-element.148), channel_id=1, source_target_pairs={{16,0},{32,16},{48,32},{64,48},{80,64},{96,80},{112,96},{128,112},... | collective-permute-start | bytes 18440 | tf_op jit(solution)/shard_map/ppermute | solution.py:18
  24.0 9.1 %copy-start.98 = (bf16[64]{0:T(256)(128)(2,1)S(1)}, bf16[64]{0:T(256)(128)(2,1)}, u32[]{:S(2)}) copy-start(bf16[64]{0:T(256)(128)(2,1)} %param.23) | copy-start | bytes 388
  24.7 65.4 %copy-start.28 = (f32[64]{0:T(128)}, f32[64]{0:T(128)S(1)}, u32[]{:S(2)}) copy-start(f32[64]{0:T(128)S(1)} %get-tuple-element.189) | copy-start | bytes 772
  24.7 65.4 %copy-start.30 = (f32[64]{0:T(128)}, f32[64]{0:T(128)S(1)}, u32[]{:S(2)}) copy-start(f32[64]{0:T(128)S(1)} %get-tuple-element.190) | copy-start | bytes 772
  24.7 65.4 %copy-start.32 = (f32[64]{0:T(128)}, f32[64]{0:T(128)S(1)}, u32[]{:S(2)}) copy-start(f32[64]{0:T(128)S(1)} %get-tuple-element.191) | copy-start | bytes 772
  24.7 65.4 %copy-start.34 = (f32[64]{0:T(128)}, f32[64]{0:T(128)S(1)}, u32[]{:S(2)}) copy-start(f32[64]{0:T(128)S(1)} %get-tuple-element.192) | copy-start | bytes 772
  24.7 65.4 %copy-start.36 = (f32[64]{0:T(128)}, f32[64]{0:T(128)S(1)}, u32[]{:S(2)}) copy-start(f32[64]{0:T(128)S(1)} %get-tuple-element.193) | copy-start | bytes 772
  24.7 65.4 %copy-start.38 = (f32[64]{0:T(128)}, f32[64]{0:T(128)S(1)}, u32[]{:S(2)}) copy-start(f32[64]{0:T(128)S(1)} %get-tuple-element.194) | copy-start | bytes 772
  24.7 65.4 %copy-start.40 = (f32[64]{0:T(128)}, f32[64]{0:T(128)S(1)}, u32[]{:S(2)}) copy-start(f32[64]{0:T(128)S(1)} %get-tuple-element.195) | copy-start | bytes 772
  24.8 65.4 %copy-start.42 = (f32[64]{0:T(128)}, f32[64]{0:T(128)S(1)}, u32[]{:S(2)}) copy-start(f32[64]{0:T(128)S(1)} %get-tuple-element.196) | copy-start | bytes 772
  24.8 65.4 %copy-start.44 = (f32[64]{0:T(128)}, f32[64]{0:T(128)S(1)}, u32[]{:S(2)}) copy-start(f32[64]{0:T(128)S(1)} %get-tuple-element.197) | copy-start | bytes 772
  24.8 65.4 %copy-start.46 = (f32[64]{0:T(128)}, f32[64]{0:T(128)S(1)}, u32[]{:S(2)}) copy-start(f32[64]{0:T(128)S(1)} %get-tuple-element.198) | copy-start | bytes 772
  24.8 65.4 %copy-start.48 = (f32[64]{0:T(128)}, f32[64]{0:T(128)S(1)}, u32[]{:S(2)}) copy-start(f32[64]{0:T(128)S(1)} %get-tuple-element.199) | copy-start | bytes 772
  25.4 64.8 %copy-start.50 = (f32[64]{0:T(128)}, f32[64]{0:T(128)S(1)}, u32[]{:S(2)}) copy-start(f32[64]{0:T(128)S(1)} %get-tuple-element.151) | copy-start | bytes 772
  25.4 64.8 %copy-start.52 = (f32[64]{0:T(128)}, f32[64]{0:T(128)S(1)}, u32[]{:S(2)}) copy-start(f32[64]{0:T(128)S(1)} %get-tuple-element.152) | copy-start | bytes 772
  25.4 64.8 %copy-start.54 = (f32[64]{0:T(128)}, f32[64]{0:T(128)S(1)}, u32[]{:S(2)}) copy-start(f32[64]{0:T(128)S(1)} %get-tuple-element.153) | copy-start | bytes 772
  25.4 64.8 %copy-start.56 = (f32[64]{0:T(128)}, f32[64]{0:T(128)S(1)}, u32[]{:S(2)}) copy-start(f32[64]{0:T(128)S(1)} %get-tuple-element.154) | copy-start | bytes 772
  25.4 64.8 %copy-start.58 = (f32[64]{0:T(128)}, f32[64]{0:T(128)S(1)}, u32[]{:S(2)}) copy-start(f32[64]{0:T(128)S(1)} %get-tuple-element.155) | copy-start | bytes 772
  25.4 64.8 %copy-start.60 = (f32[64]{0:T(128)}, f32[64]{0:T(128)S(1)}, u32[]{:S(2)}) copy-start(f32[64]{0:T(128)S(1)} %get-tuple-element.156) | copy-start | bytes 772
  25.4 64.8 %copy-start.62 = (f32[64]{0:T(128)}, f32[64]{0:T(128)S(1)}, u32[]{:S(2)}) copy-start(f32[64]{0:T(128)S(1)} %get-tuple-element.157) | copy-start | bytes 772
  25.5 64.8 %copy-start.64 = (f32[64]{0:T(128)}, f32[64]{0:T(128)S(1)}, u32[]{:S(2)}) copy-start(f32[64]{0:T(128)S(1)} %get-tuple-element.158) | copy-start | bytes 772
  25.5 64.8 %copy-start.66 = (f32[64]{0:T(128)}, f32[64]{0:T(128)S(1)}, u32[]{:S(2)}) copy-start(f32[64]{0:T(128)S(1)} %get-tuple-element.159) | copy-start | bytes 772
  25.5 64.8 %copy-start.68 = (f32[64]{0:T(128)}, f32[64]{0:T(128)S(1)}, u32[]{:S(2)}) copy-start(f32[64]{0:T(128)S(1)} %get-tuple-element.160) | copy-start | bytes 772
  25.5 64.8 %copy-start.70 = (f32[64]{0:T(128)}, f32[64]{0:T(128)S(1)}, u32[]{:S(2)}) copy-start(f32[64]{0:T(128)S(1)} %get-tuple-element.161) | copy-start | bytes 772
  25.5 64.8 %copy-start.72 = (f32[64]{0:T(128)}, f32[64]{0:T(128)S(1)}, u32[]{:S(2)}) copy-start(f32[64]{0:T(128)S(1)} %get-tuple-element.162) | copy-start | bytes 772
  25.5 64.8 %copy-start.74 = (f32[64]{0:T(128)}, f32[64]{0:T(128)S(1)}, u32[]{:S(2)}) copy-start(f32[64]{0:T(128)S(1)} %get-tuple-element.163) | copy-start | bytes 772
  26.8 82.9 %copy-start.18 = (f32[2048]{0:T(1024)}, f32[2048]{0:T(1024)S(1)}, u32[]{:S(2)}) copy-start(f32[2048]{0:T(1024)S(1)} %get-tuple-element.201) | copy-start | bytes 24580
  27.0 62.2 %collective-permute-start.3 = (bf16[1,64,3,134]{1,2,3,0:T(4,128)(2,1)S(1)}, bf16[1,64,3,134]{1,2,3,0:T(4,128)(2,1)S(1)}, u32[]{:S(2)}, u32[]{:S(2)}) collective-permute-start(bf16[1,64,3,134]{1,2,3,0:T(4,128)(2,1)S(1)} %get-tuple-element.144), channel_id=1, source_target_pairs={{1,0},{2,1},{3,2},{4,3},{5,4},{6,5},{7,6},{8,7},{9,8},{10,9},{11,1... | collective-permute-start | bytes 154376 | tf_op jit(solution)/shard_map/ppermute | solution.py:18
  33.5 56.1 %collective-permute-start.2 = (bf16[1,64,3,134]{1,2,3,0:T(4,128)(2,1)S(1)}, bf16[1,64,3,134]{1,2,3,0:T(4,128)(2,1)S(1)}, u32[]{:S(2)}, u32[]{:S(2)}) collective-permute-start(bf16[1,64,3,134]{1,2,3,0:T(4,128)(2,1)S(1)} %get-tuple-element.143), channel_id=1, source_target_pairs={{0,1},{1,2},{2,3},{3,4},{4,5},{5,6},{6,7},{7,8},{8,9},{9,10},{10,1... | collective-permute-start | bytes 154376 | tf_op jit(solution)/shard_map/ppermute | solution.py:16
  120.2 6.9 %collective-permute-start.4 = (bf16[1,64,16,3]{3,1,2,0:T(8,128)(2,1)S(1)}, bf16[1,64,16,3]{3,1,2,0:T(8,128)(2,1)S(1)}, u32[]{:S(2)}, u32[]{:S(2)}) collective-permute-start(bf16[1,64,16,3]{3,1,2,0:T(8,128)(2,1)S(1)} %get-tuple-element.149), channel_id=1, source_target_pairs={{0,16},{16,32},{32,48},{48,64},{64,80},{80,96},{96,112},{112,128},... | collective-permute-start | bytes 18440 | tf_op jit(solution)/shard_map/ppermute | solution.py:16
  123.3 15.1 %copy-start.5 = (f32[1,64,16,128]{3,2,1,0:T(8,128)S(1)}, f32[1,64,16,128]{3,2,1,0:T(8,128)}, u32[]{:S(2)}) copy-start(f32[1,64,16,128]{3,2,1,0:T(8,128)} %copy.108) | copy-start | bytes 1572868
  123.3 15.1 %copy-start.7 = (bf16[256,2048]{0,1:T(8,128)(2,1)S(1)}, bf16[256,2048]{0,1:T(8,128)(2,1)}, u32[]{:S(2)}) copy-start(bf16[256,2048]{0,1:T(8,128)(2,1)} %get-tuple-element.205) | copy-start | bytes 3145732
  123.4 15.1 %copy-start.15 = (f32[1,64,16,128]{3,2,1,0:T(8,128)S(1)}, f32[1,64,16,128]{3,2,1,0:T(8,128)}, u32[]{:S(2)}) copy-start(f32[1,64,16,128]{3,2,1,0:T(8,128)} %copy.95) | copy-start | bytes 1572868
  123.4 15.1 %copy-start.19 = (f32[2048]{0:T(1024)S(1)}, f32[2048]{0:T(1024)}, u32[]{:S(2)}) copy-start(f32[2048]{0:T(1024)} %copy-done.18) | copy-start | bytes 24580
  123.4 15.1 %copy-start.22 = (bf16[64,256]{1,0:T(8,128)(2,1)S(1)}, bf16[64,256]{1,0:T(8,128)(2,1)}, u32[]{:S(2)}) copy-start(bf16[64,256]{1,0:T(8,128)(2,1)} %param.22) | copy-start | bytes 98308
  123.4 15.1 %copy-start.87 = (f32[64]{0:T(128)S(1)}, f32[64]{0:T(128)}, u32[]{:S(2)}) copy-start(f32[64]{0:T(128)} %convert_element_type.420) | copy-start | bytes 772
  123.4 11.0 %collective-permute-start.5 = (bf16[1,64,16,3]{3,1,2,0:T(8,128)(2,1)S(1)}, bf16[1,64,16,3]{3,1,2,0:T(8,128)(2,1)S(1)}, u32[]{:S(2)}, u32[]{:S(2)}) collective-permute-start(bf16[1,64,16,3]{3,1,2,0:T(8,128)(2,1)S(1)} %get-tuple-element.150), channel_id=1, source_target_pairs={{16,0},{32,16},{48,32},{64,48},{80,64},{96,80},{112,96},{128,112},... | collective-permute-start | bytes 18440 | tf_op jit(solution)/shard_map/ppermute | solution.py:18
  127.1 12.6 %copy-start.3 = (f32[2048,64]{0,1:T(8,128)S(1)}, f32[2048,64]{0,1:T(8,128)}, u32[]{:S(2)}) copy-start(f32[2048,64]{0,1:T(8,128)} %copy-done.2) | copy-start | bytes 1572868
  135.2 10.0 %collective-permute-start.6 = (bf16[1,64,3,134]{3,1,2,0:T(8,128)(2,1)}, bf16[1,64,3,134]{3,1,2,0:T(8,128)(2,1)}, u32[]{:S(2)}, u32[]{:S(2)}) collective-permute-start(bf16[1,64,3,134]{3,1,2,0:T(8,128)(2,1)} %get-tuple-element.140), channel_id=1, source_target_pairs={{0,1},{1,2},{2,3},{3,4},{4,5},{5,6},{6,7},{7,8},{8,9},{9,10},{10,1... | collective-permute-start | bytes 154376 | tf_op jit(solution)/shard_map/ppermute | solution.py:16
  137.2 8.1 %collective-permute-start.7 = (bf16[1,64,3,134]{3,1,2,0:T(8,128)(2,1)}, bf16[1,64,3,134]{3,1,2,0:T(8,128)(2,1)}, u32[]{:S(2)}, u32[]{:S(2)}) collective-permute-start(bf16[1,64,3,134]{3,1,2,0:T(8,128)(2,1)} %get-tuple-element.139), channel_id=1, source_target_pairs={{1,0},{2,1},{3,2},{4,3},{5,4},{6,5},{7,6},{8,7},{9,8},{10,9},{11,1... | collective-permute-start | bytes 154376 | tf_op jit(solution)/shard_map/ppermute | solution.py:18
  141.1 7.4 %copy-start.37 = (f32[64]{0:T(128)S(1)}, f32[64]{0:T(128)}, u32[]{:S(2)}) copy-start(f32[64]{0:T(128)} %copy-done.36) | copy-start | bytes 772
  141.1 7.4 %copy-start.39 = (f32[64]{0:T(128)S(1)}, f32[64]{0:T(128)}, u32[]{:S(2)}) copy-start(f32[64]{0:T(128)} %copy-done.38) | copy-start | bytes 772
  141.1 7.4 %copy-start.41 = (f32[64]{0:T(128)S(1)}, f32[64]{0:T(128)}, u32[]{:S(2)}) copy-start(f32[64]{0:T(128)} %copy-done.40) | copy-start | bytes 772
  141.1 7.4 %copy-start.43 = (f32[64]{0:T(128)S(1)}, f32[64]{0:T(128)}, u32[]{:S(2)}) copy-start(f32[64]{0:T(128)} %copy-done.42) | copy-start | bytes 772
  141.1 7.4 %copy-start.45 = (f32[64]{0:T(128)S(1)}, f32[64]{0:T(128)}, u32[]{:S(2)}) copy-start(f32[64]{0:T(128)} %copy-done.44) | copy-start | bytes 772
  141.1 7.4 %copy-start.47 = (f32[64]{0:T(128)S(1)}, f32[64]{0:T(128)}, u32[]{:S(2)}) copy-start(f32[64]{0:T(128)} %copy-done.46) | copy-start | bytes 772
  141.2 7.4 %copy-start.49 = (f32[64]{0:T(128)S(1)}, f32[64]{0:T(128)}, u32[]{:S(2)}) copy-start(f32[64]{0:T(128)} %copy-done.48) | copy-start | bytes 772
  141.2 7.4 %copy-start.51 = (f32[64]{0:T(128)S(1)}, f32[64]{0:T(128)}, u32[]{:S(2)}) copy-start(f32[64]{0:T(128)} %copy-done.50) | copy-start | bytes 772
  156.9 331.4 %all-reduce.5.cloned.1.call-start = ((), (), s32[]{:S(2)}) async-start(), calls=%async_computation.2 | async-start | bytes 262144 | tf_op jit(solution)/shard_map/psum | solution.py:179
  282.0 10.7 %copy-start.89 = (pred[128]{0:T(512)(128)(4,1)S(1)}, pred[128]{0:T(512)(128)(4,1)}, u32[]{:S(2)}) copy-start(pred[128]{0:T(512)(128)(4,1)} %get-tuple-element.131) | copy-start | bytes 388
  282.0 10.7 %copy-start.90 = (pred[128]{0:T(512)(128)(4,1)S(1)}, pred[128]{0:T(512)(128)(4,1)}, u32[]{:S(2)}) copy-start(pred[128]{0:T(512)(128)(4,1)} %get-tuple-element.204) | copy-start | bytes 388
  282.0 10.7 %copy-start.11 = (f32[1,64,19,128]{3,1,2,0:T(8,128)S(1)}, f32[1,64,19,128]{3,1,2,0:T(8,128)}, u32[]{:S(2)}) copy-start(f32[1,64,19,128]{3,1,2,0:T(8,128)} %copy-done.10) | copy-start | bytes 1867780
  282.0 10.7 %slice-start = ((f32[1,64,19,128]{3,1,2,0:T(8,128)}), f32[1,64,16,128]{3,1,2,0:T(8,128)S(1)}, s32[]{:S(2)}) async-start(f32[1,64,19,128]{3,1,2,0:T(8,128)} %copy-done.10), calls=%async_computation.3 | async-start | bytes 1048576 | tf_op jit(solution)/shard_map/slice | solution.py:167
  282.1 10.8 %copy-start.17 = (bf16[1,64,16,128]{3,2,1,0:T(8,128)(2,1)S(1)}, bf16[1,64,16,128]{3,2,1,0:T(8,128)(2,1)}, u32[]{:S(2)}) copy-start(bf16[1,64,16,128]{3,2,1,0:T(8,128)(2,1)} %param.14) | copy-start | bytes 786436
  282.1 10.8 %copy-start.23 = (f32[16,128]{1,0:T(8,128)S(1)}, f32[16,128]{1,0:T(8,128)}, u32[]{:S(2)}) copy-start(f32[16,128]{1,0:T(8,128)} %get-tuple-element.200) | copy-start | bytes 24580
  (48 other events, 263.2 us)
Sparse Core Ops, SparseCore 0:
  11.7 68.0 all-gather.2
  157.0 65.3 all-gather.4
  228.2 260.0 all-reduce.4
where the time goes:
time: 499 us; the launch traced here: 498 us
  waiting for transfers between devices  244 us (49%)
  blocking collectives  107 us (21%)
  local copies, waits for them, and re-layouts  46.1 us (9%)
  other arithmetic  45.4 us (9%)
  starting transfers between devices  24.7 us (5%)
  between operations  15.4 us (3%)
  matrix products  15.1 us (3%)
    psum x1, waiting for transfers between devices, shards(): lax.psum((g_depth, gain_gradient, g_bias, g_up_w, g_up_b, g_down, g_scale...  195 us
    psum x1, blocking collectives, shards(): lax.psum((g_depth, gain_gradient, g_bias, g_up_w, g_up_b, g_down, g_scale...  107 us
    all_gather x1, waiting for transfers between devices, shards(): lax.all_gather(upper, 'lon', axis=3, tiled=True)  42.1 us
    ppermute x4, starting transfers between devices, extended_2(): lax.ppermute(tail, axis, [(i, (i + 1) % count) for i in range(ends)])  16.4 us
    reduce_sum x4, other arithmetic, shards(): jnp.sum(d_conv_f * extended[:, :, row_tap:row_tap + rows, col_tap:col_tap...  10.9 us
    reduce_sum x1, other arithmetic, cell_terms(): mean_c = jnp.mean(conv, axis=0, keepdims=True)  9.98 us
  transfers between devices with their start and end apart: 11, of which 3 were waited for; matrix products, arithmetic and copies ran while one was open for 12% of the time, Pallas kernels for 0%

commit v1 on v0

--- a/solution.py
+++ b/solution.py
@@ -176,9 +176,8 @@
     own = own.at[:, :, rows - 3 :, :].add(jnp.where(is_top, extra, 0.0))
     grad_fields = (mask_f[None, None] * cotangent.astype(jnp.float32) + own).astype(jnp.bfloat16)
     gain_gradient, g_bias, g_up_w, g_up_b, g_down, g_scale = parts
-    summed = lax.psum(
-        (g_depth, gain_gradient, g_bias, g_up_w, g_up_b, g_down, g_scale), ("lon", "lat")
-    )
+    partial = lax.psum((g_depth, gain_gradient, g_bias, g_up_w, g_up_b, g_down, g_scale), "lon")
+    summed = lax.psum(partial, "lat")
     return (
         output,
         grad_fields,

time: 499 us -> 622 us (1.25); the launches traced: 498 us -> 612 us
  blocking collectives: 107 us -> 189 us
  waiting for transfers between devices: 244 us -> 283 us
  local copies, waits for them, and re-layouts: 46.1 us -> 39.1 us
    psum x1, waiting for transfers between devices: 195 us -> 56.4 us  [shards(): lax.psum((g_depth, gain_gradient, g_bias, g_up_w, g_up_b, g_down, g_scale...]
    psum x0 -> x1, waiting for transfers between devices: none -> 111 us  [shards(): summed = lax.psum(partial, 'lat')]
    all_gather x1, waiting for transfers between devices: 0.01 us -> 61.5 us  [shards(): lax.all_gather(margin.astype(jnp.bfloat16), 'lon', axis=3, tiled=True)]
    psum x0 -> x1, blocking collectives: none -> 48.9 us  [shards(): summed = lax.psum(partial, 'lat')]
    psum x1, blocking collectives: 107 us -> 140 us  [shards(): lax.psum((g_depth, gain_gradient, g_bias, g_up_w, g_up_b, g_down, g_scale...]
  transfers between devices with their start and end apart: 11 -> 12, of which waited for: 3 -> 7; matrix products, arithmetic and copies ran while one was open for 12% -> 10% of each run, Pallas kernels for 0% -> 0%
where the time goes in v1:
time: 622 us; the launch traced here: 612 us
  waiting for transfers between devices  283 us (45%)
  blocking collectives  189 us (30%)
  other arithmetic  44.5 us (7%)
  local copies, waits for them, and re-layouts  39.1 us (6%)
  starting transfers between devices  24.9 us (4%)
  matrix products  15.7 us (3%)
  between operations  15.4 us (2%)
    psum x1, blocking collectives, shards(): lax.psum((g_depth, gain_gradient, g_bias, g_up_w, g_up_b, g_down, g_scale...  140 us
    psum x1, waiting for transfers between devices, shards(): summed = lax.psum(partial, 'lat')  111 us
    all_gather x1, waiting for transfers between devices, shards(): lax.all_gather(margin.astype(jnp.bfloat16), 'lon', axis=3, tiled=True)  61.5 us
    psum x1, waiting for transfers between devices, shards(): lax.psum((g_depth, gain_gradient, g_bias, g_up_w, g_up_b, g_down, g_scale...  56.4 us
    psum x1, blocking collectives, shards(): summed = lax.psum(partial, 'lat')  48.9 us
    all_gather x1, waiting for transfers between devices, shards(): lax.all_gather(upper, 'lon', axis=3, tiled=True)  42.4 us
    ppermute x4, starting transfers between devices, extended_2(): lax.ppermute(tail, axis, [(i, (i + 1) % count) for i in range(ends)])  16.7 us
  transfers between devices with their start and end apart: 12, of which 7 were waited for; matrix products, arithmetic and copies ran while one was open for 10% of the time, Pallas kernels for 0%

profile of v1, /device:TPU:1, one launch (start us, length us, event | category | flops | bytes accessed | tf_op | source)
XLA Modules:
  0.0 611.8 jit_solution(16386909613917631834)
XLA Ops:
  7.3 1.0 slice.730
  8.3 0.6 rev.6
  9.0 1.5 copy.94
  10.5 7.2 %collective-permute-start = (bf16[1,64,16,3]{1,2,3,0:T(8,128)(2,1)S(1)}, bf16[1,64,16,3]{1,2,3,0:T(8,128)(2,1)S(1)}, u32[]{:S(2)}, u32[]{:S(2)}) collective-permute-start(bf16[1,64,16,3]{1,2,3,0:T(8,128)(2,1)S(1)} %get-tuple-element.154), channel_id=1, source_target_pairs={{0,16},{16,32},{32,48},{48,64},{64,80},{80,96},{96,112},{112,128},... | collective-permute-start | bytes 18440 | tf_op jit(solution)/shard_map/ppermute | solution.py:16
  17.7 3.5 collective-permute-start.1
  21.3 0.7 convert_element_type.421
  22.0 2.0 gather_fusion
  24.0 0.7 compare_and_fusion
  25.0 0.6 slice_bitcast_fusion.47
  25.7 0.6 fusion.138
  26.6 1.3 collective-permute-start.3
  27.9 0.6 pad_clamp_fusion
  28.5 1.4 copy.95
  29.9 0.5 convert_element_type.471
  30.4 0.5 convert_element_type.472
  30.9 1.1 copy.108
  32.0 0.5 convert_element_type.420
  32.5 4.2 collective-permute-start.2
  36.7 42.4 %all-gather.3.cloned.1.call-done = bf16[1,64,3,4096]{3,1,2,0:T(8,128)(2,1)} async-done(((bf16[1,64,3,128]{3,1,2,0:T(8,128)(2,1)}), bf16[1,64,3,4096]{3,1,2,0:T(8,128)(2,1)}) %all-gather.3.cloned.1.call-update) | async-done | bytes 1572880 | tf_op jit(solution)/shard_map/all_gather | solution.py:116
  79.1 6.4 %copy.102 = bf16[1,64,3,4096]{1,2,3,0:T(4,128)(2,1)} copy(bf16[1,64,3,4096]{3,1,2,0:T(8,128)(2,1)} %all-gather.3.cloned.1.call-done) | data formatting | bytes 3145728 | tf_op jit(solution)/shard_map/all_gather | solution.py:116
  85.5 3.0 gather_fusion.1
  88.4 0.4 fusion.126
  88.8 0.5 maximum_maximum_fusion
  89.7 10.5 %fusion.134 = (f32[16,128]{0,1:T(8,128)S(1)}, f32[1,64,16,128]{1,2,3,0:T(8,128)S(1)}) fusion(bf16[1,64,19,134]{1,2,3,0:T(8,128)(2,1)S(1)} %get-tuple-element.149, f32[64]{0:T(128)S(1)} %get-tuple-element.159, f32[64]{0:T(128)S(1)} %get-tuple-element.160, f32[64]{0:T(128)S(1)} %get-tuple-element.161, f32[64]{0:T(128)S(1)} %get-tuple-element.162, ...), kind=kLoop, calls=%fused_computation.375 | loop fusion | flops 20051968 | bytes 11829504 | tf_op jit(solution)/shard_map/reduce_sum | solution.py:33
  100.2 1.4 copy.103
  101.8 0.6 multiply_reduce_fusion
  102.5 6.9 %fusion.5 = (bf16[256,2048]{0,1:T(8,128)(2,1)}, f32[256,2048]{0,1:T(8,128)S(1)}) fusion(f32[256]{0:T(256)S(1)} %convert_element_type.474, bf16[256,64]{0,1:T(8,128)(2,1)S(1)} %copy-done, f32[64]{0:T(128)} %convert_element_type.472, f32[64]{0:T(128)} %convert_element_type.471, f32[2048]{0:T(1024)S(1)} %rsqrt_bitcast_fusion, ...), kind=kOutput, calls=%fused_computation.63 | convolution fusion | flops 102367232 | bytes 3720704 | tf_op jit(solution)/shard_map/dot_general | solution.py:43
  109.5 2.0 convert_reduce_fusion
  111.5 1.8 fusion.121
  113.4 0.9 fusion.123
  114.4 0.7 copy-done.11
  115.1 0.5 copy.114
  115.6 1.0 copy.109
  116.6 4.4 fusion.113
  121.2 3.3 collective-permute-start.4
  124.5 1.9 collective-permute-start.5
  126.4 1.7 fusion.133
  128.2 7.2 %collective-permute-done.5 = bf16[1,64,16,3]{3,1,2,0:T(8,128)(2,1)S(1)} collective-permute-done((bf16[1,64,16,3]{3,1,2,0:T(8,128)(2,1)S(1)}, bf16[1,64,16,3]{3,1,2,0:T(8,128)(2,1)S(1)}, u32[]{:S(2)}, u32[]{:S(2)}) %collective-permute-start.5) | collective-permute-done | bytes 6176 | tf_op jit(solution)/shard_map/ppermute | solution.py:18
  135.3 0.8 pad_maximum_fusion.8
  136.2 2.1 collective-permute-start.6
  138.2 1.3 collective-permute-start.7
  139.6 1.0 fusion.132
  140.7 4.2 collective-permute-done.7
  144.8 1.4 pad_maximum_fusion.1
  146.3 1.4 pad_maximum_fusion.2
  147.8 7.0 %multiply_add_fusion = f32[1,64,19,128]{3,1,2,0:T(8,128)S(1)} fusion(bf16[1,64,19,134]{3,1,2,0:T(8,128)(2,1)S(1)} %get-tuple-element.145, bf16[1,64,22,134]{3,1,2,0:T(8,128)(2,1)S(1)} %pad_maximum_fusion.1, bf16[1,64,19,134]{3,1,2,0:T(8,128)(2,1)S(1)} %get-tuple-element.144, f32[64]{0:T(128)} %copy-done.38, f32[64]{0:T(128)} %copy-done.39, ...), kind=kLoop, calls=%fused_computation.239 | loop fusion | flops 22724608 | bytes 10072832 | tf_op jit(solution)/shard_map/add | solution.py:164
  154.8 0.9 copy-done.9
  155.6 0.6 slice.1226
  156.3 2.2 multiply_reduce_fusion.1
  158.9 0.7 copy.119
  159.6 1.0 fusion.112
  160.9 1.2 fusion.92
  162.2 3.3 fusion.85
  165.7 140.5 %all-reduce.1 = (f32[64,7,7]{0,2,1:T(8,128)S(1)}, f32[64]{0:T(128)S(1)}, f32[64]{0:T(128)S(1)}, f32[256]{0:T(256)S(1)}, f32[64]{0:T(128)S(1)}) all-reduce(f32[64,7,7]{0,2,1:T(8,128)S(1)} %constant_dynamic-update-slice_fusion, f32[64]{0:T(128)S(1)} %copy-done.87, f32[64]{0:T(128)S(1)} %reduce_sum.567, ...), channel_id=1, replica_groups=mesh['lon'=32,'lat'=16] {'lon'}, use_global_device_ids=true, to_apply=%region_53.54 | all-reduce | flops 3584 | bytes 28672 | tf_op jit(solution)/shard_map/psum | solution.py:179
  306.2 48.9 %all-reduce.3 = (f32[64,7,7]{0,2,1:T(8,128)}, f32[64]{0:T(128)}, f32[64]{0:T(128)}, f32[256]{0:T(256)}, f32[64]{0:T(128)}) all-reduce(f32[64,7,7]{0,2,1:T(8,128)S(1)} %get-tuple-element.124, f32[64]{0:T(128)S(1)} %get-tuple-element.125, f32[64]{0:T(128)S(1)} %get-tuple-element.126, ...), channel_id=1, replica_groups=mesh['lon'=32,'lat'=16] {'lat'}, use_global_device_ids=true, to_apply=%region_54.55 | all-reduce | flops 3584 | bytes 28672 | tf_op jit(solution)/shard_map/psum | solution.py:180
  355.1 56.4 %all-reduce.8.cloned.1.call-done = (f32[256,64]{0,1:T(8,128)}, f32[64,256]{1,0:T(8,128)}) async-done(((f32[256,64]{0,1:T(8,128)}, f32[64,256]{1,0:T(8,128)}), (f32[256,64]{0,1:T(8,128)}, f32[64,256]{1,0:T(8,128)})) %all-reduce.8.cloned.1.call-update) | async-done | bytes 131088 | tf_op jit(solution)/shard_map/psum | solution.py:179
  411.5 61.5 %all-gather.5.cloned.1.call-done = bf16[1,64,3,4096]{3,1,2,0:T(8,128)(2,1)} async-done(((bf16[1,64,3,128]{3,1,2,0:T(8,128)(2,1)}), bf16[1,64,3,4096]{3,1,2,0:T(8,128)(2,1)}) %all-gather.5.cloned.1.call-update) | async-done | bytes 1572880 | tf_op jit(solution)/shard_map/all_gather | solution.py:173
  473.0 6.4 %copy.112 = bf16[1,64,3,4096]{1,2,3,0:T(4,128)(2,1)} copy(bf16[1,64,3,4096]{3,1,2,0:T(8,128)(2,1)} %all-gather.5.cloned.1.call-done) | data formatting | bytes 3145728 | tf_op jit(solution)/shard_map/all_gather | solution.py:173
  479.4 6.2 %bitcast_convert_fusion = f32[64,3,4096]{0,1,2:T(4,128)} fusion(bf16[1,64,3,4096]{1,2,3,0:T(4,128)(2,1)} %copy.112), kind=kLoop, calls=%fused_computation.52 | loop fusion | flops 786432 | bytes 4718592 | tf_op jit(solution)/shard_map/convert_element_type | solution.py:173
  485.7 4.3 gather_fusion.2
  490.3 0.9 copy.115
  491.2 111.1 %all-reduce.10.cloned.1.call-done = (f32[256,64]{0,1:T(8,128)}, f32[64,256]{1,0:T(8,128)}) async-done(((f32[256,64]{0,1:T(8,128)}, f32[64,256]{1,0:T(8,128)}), (f32[256,64]{0,1:T(8,128)}, f32[64,256]{1,0:T(8,128)})) %all-reduce.10.cloned.1.call-update) | async-done | bytes 131088 | tf_op jit(solution)/shard_map/psum | solution.py:180
  602.3 1.5 copy.161
  603.8 1.5 copy.162
  (240 shorter events, 2.0 us)
Async XLA Ops:
  7.2 95.3 %copy-start = (bf16[256,64]{0,1:T(8,128)(2,1)S(1)}, bf16[256,64]{0,1:T(8,128)(2,1)}, u32[]{:S(2)}) copy-start(bf16[256,64]{0,1:T(8,128)(2,1)} %param.20) | copy-start | bytes 98308
  7.2 18.4 %copy-start.23 = (s32[16,128]{1,0:T(8,128)S(1)}, s32[16,128]{1,0:T(8,128)}, u32[]{:S(2)}) copy-start(s32[16,128]{1,0:T(8,128)} %param.15) | copy-start | bytes 24580
  7.2 19.1 %copy-start.16 = (bf16[1,64,16,128]{3,2,1,0:T(8,128)(2,1)S(1)}, bf16[1,64,16,128]{3,2,1,0:T(8,128)(2,1)}, u32[]{:S(2)}) copy-start(bf16[1,64,16,128]{3,2,1,0:T(8,128)(2,1)} %param.14) | copy-start | bytes 786436
  7.2 71.9 %all-gather.3.cloned.1.call-start = ((), (), s32[]{:S(2)}) async-start(), calls=%async_computation | async-start | bytes 1622016 | tf_op jit(solution)/shard_map/all_gather | solution.py:116
  8.9 402.6 %all-reduce.8.cloned.1.call-start = ((), (), s32[]{:S(2)}) async-start(), calls=%async_computation.2 | async-start | bytes 262144 | tf_op jit(solution)/shard_map/psum | solution.py:179
  10.5 19.4 %copy-start.89 = (bf16[64]{0:T(256)(128)(2,1)S(1)}, bf16[64]{0:T(256)(128)(2,1)}, u32[]{:S(2)}) copy-start(bf16[64]{0:T(256)(128)(2,1)} %param.18) | copy-start | bytes 388
  10.5 19.9 %copy-start.90 = (bf16[64]{0:T(256)(128)(2,1)S(1)}, bf16[64]{0:T(256)(128)(2,1)}, u32[]{:S(2)}) copy-start(bf16[64]{0:T(256)(128)(2,1)} %param.19) | copy-start | bytes 388
  10.5 20.4 %copy-start.91 = (bf16[256]{0:T(256)(128)(2,1)S(1)}, bf16[256]{0:T(256)(128)(2,1)}, u32[]{:S(2)}) copy-start(bf16[256]{0:T(256)(128)(2,1)} %param.21) | copy-start | bytes 1540
  10.5 15.9 %collective-permute-start = (bf16[1,64,16,3]{1,2,3,0:T(8,128)(2,1)S(1)}, bf16[1,64,16,3]{1,2,3,0:T(8,128)(2,1)S(1)}, u32[]{:S(2)}, u32[]{:S(2)}) collective-permute-start(bf16[1,64,16,3]{1,2,3,0:T(8,128)(2,1)S(1)} %get-tuple-element.154), channel_id=1, source_target_pairs={{0,16},{16,32},{32,48},{48,64},{64,80},{80,96},{96,112},{112,128},... | collective-permute-start | bytes 18440 | tf_op jit(solution)/shard_map/ppermute | solution.py:16
  17.7 8.7 %collective-permute-start.1 = (bf16[1,64,16,3]{1,2,3,0:T(8,128)(2,1)S(1)}, bf16[1,64,16,3]{1,2,3,0:T(8,128)(2,1)S(1)}, u32[]{:S(2)}, u32[]{:S(2)}) collective-permute-start(bf16[1,64,16,3]{1,2,3,0:T(8,128)(2,1)S(1)} %get-tuple-element.155), channel_id=1, source_target_pairs={{16,0},{32,16},{48,32},{64,48},{80,64},{96,80},{112,96},{128,112},... | collective-permute-start | bytes 18440 | tf_op jit(solution)/shard_map/ppermute | solution.py:18
  24.7 64.6 %copy-start.24 = (f32[64]{0:T(128)}, f32[64]{0:T(128)S(1)}, u32[]{:S(2)}) copy-start(f32[64]{0:T(128)S(1)} %get-tuple-element.196) | copy-start | bytes 772
  24.7 64.6 %copy-start.26 = (f32[64]{0:T(128)}, f32[64]{0:T(128)S(1)}, u32[]{:S(2)}) copy-start(f32[64]{0:T(128)S(1)} %get-tuple-element.197) | copy-start | bytes 772
  24.7 64.6 %copy-start.28 = (f32[64]{0:T(128)}, f32[64]{0:T(128)S(1)}, u32[]{:S(2)}) copy-start(f32[64]{0:T(128)S(1)} %get-tuple-element.198) | copy-start | bytes 772
  24.7 64.6 %copy-start.29 = (f32[64]{0:T(128)}, f32[64]{0:T(128)S(1)}, u32[]{:S(2)}) copy-start(f32[64]{0:T(128)S(1)} %get-tuple-element.199) | copy-start | bytes 772
  24.7 64.6 %copy-start.30 = (f32[64]{0:T(128)}, f32[64]{0:T(128)S(1)}, u32[]{:S(2)}) copy-start(f32[64]{0:T(128)S(1)} %get-tuple-element.200) | copy-start | bytes 772
  24.7 64.6 %copy-start.31 = (f32[64]{0:T(128)}, f32[64]{0:T(128)S(1)}, u32[]{:S(2)}) copy-start(f32[64]{0:T(128)S(1)} %get-tuple-element.201) | copy-start | bytes 772
  24.8 64.6 %copy-start.32 = (f32[64]{0:T(128)}, f32[64]{0:T(128)S(1)}, u32[]{:S(2)}) copy-start(f32[64]{0:T(128)S(1)} %get-tuple-element.202) | copy-start | bytes 772
  24.8 64.6 %copy-start.33 = (f32[64]{0:T(128)}, f32[64]{0:T(128)S(1)}, u32[]{:S(2)}) copy-start(f32[64]{0:T(128)S(1)} %get-tuple-element.203) | copy-start | bytes 772
  24.8 64.6 %copy-start.34 = (f32[64]{0:T(128)}, f32[64]{0:T(128)S(1)}, u32[]{:S(2)}) copy-start(f32[64]{0:T(128)S(1)} %get-tuple-element.204) | copy-start | bytes 772
  24.8 64.6 %copy-start.35 = (f32[64]{0:T(128)}, f32[64]{0:T(128)S(1)}, u32[]{:S(2)}) copy-start(f32[64]{0:T(128)S(1)} %get-tuple-element.205) | copy-start | bytes 772
  24.8 64.6 %copy-start.36 = (f32[64]{0:T(128)}, f32[64]{0:T(128)S(1)}, u32[]{:S(2)}) copy-start(f32[64]{0:T(128)S(1)} %get-tuple-element.206) | copy-start | bytes 772
  24.8 64.6 %copy-start.37 = (f32[64]{0:T(128)}, f32[64]{0:T(128)S(1)}, u32[]{:S(2)}) copy-start(f32[64]{0:T(128)S(1)} %get-tuple-element.158) | copy-start | bytes 772
  24.8 64.6 %copy-start.38 = (f32[64]{0:T(128)}, f32[64]{0:T(128)S(1)}, u32[]{:S(2)}) copy-start(f32[64]{0:T(128)S(1)} %get-tuple-element.159) | copy-start | bytes 772
  24.8 64.6 %copy-start.39 = (f32[64]{0:T(128)}, f32[64]{0:T(128)S(1)}, u32[]{:S(2)}) copy-start(f32[64]{0:T(128)S(1)} %get-tuple-element.160) | copy-start | bytes 772
  24.9 64.6 %copy-start.40 = (f32[64]{0:T(128)}, f32[64]{0:T(128)S(1)}, u32[]{:S(2)}) copy-start(f32[64]{0:T(128)S(1)} %get-tuple-element.161) | copy-start | bytes 772
  24.9 64.6 %copy-start.41 = (f32[64]{0:T(128)}, f32[64]{0:T(128)S(1)}, u32[]{:S(2)}) copy-start(f32[64]{0:T(128)S(1)} %get-tuple-element.162) | copy-start | bytes 772
  24.9 64.6 %copy-start.42 = (f32[64]{0:T(128)}, f32[64]{0:T(128)S(1)}, u32[]{:S(2)}) copy-start(f32[64]{0:T(128)S(1)} %get-tuple-element.163) | copy-start | bytes 772
  24.9 64.6 %copy-start.43 = (f32[64]{0:T(128)}, f32[64]{0:T(128)S(1)}, u32[]{:S(2)}) copy-start(f32[64]{0:T(128)S(1)} %get-tuple-element.164) | copy-start | bytes 772
  24.9 64.6 %copy-start.44 = (f32[64]{0:T(128)}, f32[64]{0:T(128)S(1)}, u32[]{:S(2)}) copy-start(f32[64]{0:T(128)S(1)} %get-tuple-element.165) | copy-start | bytes 772
  24.9 64.6 %copy-start.45 = (f32[64]{0:T(128)}, f32[64]{0:T(128)S(1)}, u32[]{:S(2)}) copy-start(f32[64]{0:T(128)S(1)} %get-tuple-element.166) | copy-start | bytes 772
  24.9 64.6 %copy-start.46 = (f32[64]{0:T(128)}, f32[64]{0:T(128)S(1)}, u32[]{:S(2)}) copy-start(f32[64]{0:T(128)S(1)} %get-tuple-element.167) | copy-start | bytes 772
  24.9 64.6 %copy-start.47 = (f32[64]{0:T(128)}, f32[64]{0:T(128)S(1)}, u32[]{:S(2)}) copy-start(f32[64]{0:T(128)S(1)} %get-tuple-element.168) | copy-start | bytes 772
  24.9 64.6 %copy-start.48 = (f32[64]{0:T(128)}, f32[64]{0:T(128)S(1)}, u32[]{:S(2)}) copy-start(f32[64]{0:T(128)S(1)} %get-tuple-element.169) | copy-start | bytes 772
  24.9 64.6 %copy-start.49 = (f32[64]{0:T(128)}, f32[64]{0:T(128)S(1)}, u32[]{:S(2)}) copy-start(f32[64]{0:T(128)S(1)} %get-tuple-element.170) | copy-start | bytes 772
  25.0 64.6 %copy-start.50 = (f32[64]{0:T(128)}, f32[64]{0:T(128)S(1)}, u32[]{:S(2)}) copy-start(f32[64]{0:T(128)S(1)} %get-tuple-element.171) | copy-start | bytes 772
  25.0 64.6 %copy-start.51 = (f32[64]{0:T(128)}, f32[64]{0:T(128)S(1)}, u32[]{:S(2)}) copy-start(f32[64]{0:T(128)S(1)} %get-tuple-element.172) | copy-start | bytes 772
  25.0 64.6 %copy-start.52 = (f32[64]{0:T(128)}, f32[64]{0:T(128)S(1)}, u32[]{:S(2)}) copy-start(f32[64]{0:T(128)S(1)} %get-tuple-element.173) | copy-start | bytes 772
  25.0 64.6 %copy-start.53 = (f32[64]{0:T(128)}, f32[64]{0:T(128)S(1)}, u32[]{:S(2)}) copy-start(f32[64]{0:T(128)S(1)} %get-tuple-element.174) | copy-start | bytes 772
  25.0 64.6 %copy-start.54 = (f32[64]{0:T(128)}, f32[64]{0:T(128)S(1)}, u32[]{:S(2)}) copy-start(f32[64]{0:T(128)S(1)} %get-tuple-element.175) | copy-start | bytes 772
  25.0 64.6 %copy-start.55 = (f32[64]{0:T(128)}, f32[64]{0:T(128)S(1)}, u32[]{:S(2)}) copy-start(f32[64]{0:T(128)S(1)} %get-tuple-element.176) | copy-start | bytes 772
  25.6 64.0 %copy-start.56 = (f32[64]{0:T(128)}, f32[64]{0:T(128)S(1)}, u32[]{:S(2)}) copy-start(f32[64]{0:T(128)S(1)} %get-tuple-element.177) | copy-start | bytes 772
  25.7 64.0 %copy-start.57 = (f32[64]{0:T(128)}, f32[64]{0:T(128)S(1)}, u32[]{:S(2)}) copy-start(f32[64]{0:T(128)S(1)} %get-tuple-element.178) | copy-start | bytes 772
  25.7 64.0 %copy-start.58 = (f32[64]{0:T(128)}, f32[64]{0:T(128)S(1)}, u32[]{:S(2)}) copy-start(f32[64]{0:T(128)S(1)} %get-tuple-element.179) | copy-start | bytes 772
  25.7 64.0 %copy-start.59 = (f32[64]{0:T(128)}, f32[64]{0:T(128)S(1)}, u32[]{:S(2)}) copy-start(f32[64]{0:T(128)S(1)} %get-tuple-element.180) | copy-start | bytes 772
  25.7 64.0 %copy-start.60 = (f32[64]{0:T(128)}, f32[64]{0:T(128)S(1)}, u32[]{:S(2)}) copy-start(f32[64]{0:T(128)S(1)} %get-tuple-element.181) | copy-start | bytes 772
  25.7 64.0 %copy-start.61 = (f32[64]{0:T(128)}, f32[64]{0:T(128)S(1)}, u32[]{:S(2)}) copy-start(f32[64]{0:T(128)S(1)} %get-tuple-element.182) | copy-start | bytes 772
  25.7 64.0 %copy-start.62 = (f32[64]{0:T(128)}, f32[64]{0:T(128)S(1)}, u32[]{:S(2)}) copy-start(f32[64]{0:T(128)S(1)} %get-tuple-element.183) | copy-start | bytes 772
  25.7 64.0 %copy-start.63 = (f32[64]{0:T(128)}, f32[64]{0:T(128)S(1)}, u32[]{:S(2)}) copy-start(f32[64]{0:T(128)S(1)} %get-tuple-element.184) | copy-start | bytes 772
  25.7 64.0 %copy-start.64 = (f32[64]{0:T(128)}, f32[64]{0:T(128)S(1)}, u32[]{:S(2)}) copy-start(f32[64]{0:T(128)S(1)} %get-tuple-element.185) | copy-start | bytes 772
  26.6 61.8 %collective-permute-start.3 = (bf16[1,64,3,134]{1,2,3,0:T(4,128)(2,1)S(1)}, bf16[1,64,3,134]{1,2,3,0:T(4,128)(2,1)S(1)}, u32[]{:S(2)}, u32[]{:S(2)}) collective-permute-start(bf16[1,64,3,134]{1,2,3,0:T(4,128)(2,1)S(1)} %get-tuple-element.151), channel_id=1, source_target_pairs={{1,0},{2,1},{3,2},{4,3},{5,4},{6,5},{7,6},{8,7},{9,8},{10,9},{11,1... | collective-permute-start | bytes 154376 | tf_op jit(solution)/shard_map/ppermute | solution.py:18
  32.5 56.3 %collective-permute-start.2 = (bf16[1,64,3,134]{1,2,3,0:T(4,128)(2,1)S(1)}, bf16[1,64,3,134]{1,2,3,0:T(4,128)(2,1)S(1)}, u32[]{:S(2)}, u32[]{:S(2)}) collective-permute-start(bf16[1,64,3,134]{1,2,3,0:T(4,128)(2,1)S(1)} %get-tuple-element.150), channel_id=1, source_target_pairs={{0,1},{1,2},{2,3},{3,4},{4,5},{5,6},{6,7},{7,8},{8,9},{9,10},{10,1... | collective-permute-start | bytes 154376 | tf_op jit(solution)/shard_map/ppermute | solution.py:16
  121.0 18.5 %copy-start.5 = (f32[1,64,16,128]{3,2,1,0:T(8,128)S(1)}, f32[1,64,16,128]{3,2,1,0:T(8,128)}, u32[]{:S(2)}) copy-start(f32[1,64,16,128]{3,2,1,0:T(8,128)} %copy.108) | copy-start | bytes 1572868
  121.0 18.5 %copy-start.6 = (bf16[256,2048]{0,1:T(8,128)(2,1)S(1)}, bf16[256,2048]{0,1:T(8,128)(2,1)}, u32[]{:S(2)}) copy-start(bf16[256,2048]{0,1:T(8,128)(2,1)} %get-tuple-element.212) | copy-start | bytes 3145732
  121.0 18.5 %copy-start.19 = (f32[2048]{0:T(1024)S(1)}, f32[2048]{0:T(1024)}, u32[]{:S(2)}) copy-start(f32[2048]{0:T(1024)} %get-tuple-element.208) | copy-start | bytes 24580
  121.0 18.6 %copy-start.66 = (f32[64]{0:T(128)S(1)}, f32[64]{0:T(128)}, u32[]{:S(2)}) copy-start(f32[64]{0:T(128)} %convert_element_type.420) | copy-start | bytes 772
  121.2 7.0 %collective-permute-start.4 = (bf16[1,64,16,3]{3,1,2,0:T(8,128)(2,1)S(1)}, bf16[1,64,16,3]{3,1,2,0:T(8,128)(2,1)S(1)}, u32[]{:S(2)}, u32[]{:S(2)}) collective-permute-start(bf16[1,64,16,3]{3,1,2,0:T(8,128)(2,1)S(1)} %get-tuple-element.156), channel_id=1, source_target_pairs={{0,16},{16,32},{32,48},{48,64},{64,80},{80,96},{96,112},{112,128},... | collective-permute-start | bytes 18440 | tf_op jit(solution)/shard_map/ppermute | solution.py:16
  124.5 10.9 %collective-permute-start.5 = (bf16[1,64,16,3]{3,1,2,0:T(8,128)(2,1)S(1)}, bf16[1,64,16,3]{3,1,2,0:T(8,128)(2,1)S(1)}, u32[]{:S(2)}, u32[]{:S(2)}) collective-permute-start(bf16[1,64,16,3]{3,1,2,0:T(8,128)(2,1)S(1)} %get-tuple-element.157), channel_id=1, source_target_pairs={{16,0},{32,16},{48,32},{64,48},{80,64},{96,80},{112,96},{128,112},... | collective-permute-start | bytes 18440 | tf_op jit(solution)/shard_map/ppermute | solution.py:18
  136.2 4.5 collective-permute-start.6
  138.2 6.6 %collective-permute-start.7 = (bf16[1,64,3,134]{3,1,2,0:T(8,128)(2,1)}, bf16[1,64,3,134]{3,1,2,0:T(8,128)(2,1)}, u32[]{:S(2)}, u32[]{:S(2)}) collective-permute-start(bf16[1,64,3,134]{3,1,2,0:T(8,128)(2,1)} %get-tuple-element.146), channel_id=1, source_target_pairs={{1,0},{2,1},{3,2},{4,3},{5,4},{6,5},{7,6},{8,7},{9,8},{10,9},{11,1... | collective-permute-start | bytes 154376 | tf_op jit(solution)/shard_map/ppermute | solution.py:18
  140.6 332.4 %all-gather.5.cloned.1.call-start = ((), (), s32[]{:S(2)}) async-start(), calls=%async_computation.1 | async-start | bytes 1622016 | tf_op jit(solution)/shard_map/all_gather | solution.py:173
  156.3 446.0 %all-reduce.10.cloned.1.call-start = ((), (), s32[]{:S(2)}) async-start(), calls=%async_computation.3 | async-start | bytes 262144 | tf_op jit(solution)/shard_map/psum | solution.py:180
  479.4 10.7 %slice-start = ((f32[1,64,19,128]{3,1,2,0:T(8,128)}), f32[1,64,16,128]{3,1,2,0:T(8,128)S(1)}, s32[]{:S(2)}) async-start(f32[1,64,19,128]{3,1,2,0:T(8,128)} %copy-done.9), calls=%async_computation.4 | async-start | bytes 1048576 | tf_op jit(solution)/shard_map/slice | solution.py:167
  479.4 10.8 %copy-start.17 = (bf16[1,64,16,128]{3,2,1,0:T(8,128)(2,1)S(1)}, bf16[1,64,16,128]{3,2,1,0:T(8,128)(2,1)}, u32[]{:S(2)}) copy-start(bf16[1,64,16,128]{3,2,1,0:T(8,128)(2,1)} %param.14) | copy-start | bytes 786436
  479.4 10.8 %copy-start.22 = (f32[16,128]{1,0:T(8,128)S(1)}, f32[16,128]{1,0:T(8,128)}, u32[]{:S(2)}) copy-start(f32[16,128]{1,0:T(8,128)} %get-tuple-element.207) | copy-start | bytes 24580
  (42 other events, 182.1 us)
Sparse Core Ops, SparseCore 0:
  11.7 67.3 all-gather.2
  140.7 270.7 all-reduce.7
  415.6 57.3 all-gather.4
  476.1 126.1 all-reduce.9
